TPU v7x, 512 devices: a whole 4x4x16 slice. The times are simulated.
512 devices in a mesh: partner: 32 (over y, x, core), block: 16 (over z).
Axes of the slice: x: 4, y: 4, z: 16, core: 2. Of those that a mesh axis runs over, the one named last changes fastest.
Arguments:
- points: bfloat16 [32, 524288], P(None, ('partner', 'block')), may hold values from -6 to 6
- tree_order: int32 [524288], P(('partner', 'block')), may hold values from 0 to 524287, as said below
- nearby_dense_blocks: bfloat16 [4096, 3, 128, 128], P(('partner', 'block')), may hold values from -0.3125 to 0.3125
- neighbours: int32 [4096, 3], P(('partner', 'block')), may hold values from 0 to 4095, as said below
- compress: bfloat16 [4096, 128, 128], P(('partner', 'block')), may hold values from -0.5 to 0.5
- expand: bfloat16 [4096, 128, 128], P(('partner', 'block')), may hold values from -0.5 to 0.5
- top_factor: bfloat16 [4096, 128, 128], P(('partner', 'block')), may hold values from -0.5 to 0.5
- butterfly_mixers: bfloat16 [4, 4096, 2, 128, 128], P(None, ('partner', 'block')), may hold values from -0.375 to 0.375
- block_map: int32 [5, 8], replicated, may hold values from 0 to 7, as said below
Outputs:
- applied: bfloat16 [32, 524288], P(None, ('partner', 'block'))
Inputs may be any that keep to these rules, and one draw needn't show every extreme that they name: tree_order[r] lies among the 1024 points of the aligned group of 1024 rows that holds r, and names every point once. neighbours[l, 0] is l; every other entry lies within 2 leaves of l and in the same aligned group of 128 leaves as l. `block_map`: each row names exactly 4 different slots, each of them twice.
All inputs are finite; a program needn't handle non-finite values.
Results may differ from a plain program's by a relative error of at most 0.001.
Values may be sent and summed in bfloat16 or wider, within the bound.
A program may use at most 64 MiB of HBM per device.

v0:
```python
import jax
import jax.numpy as jnp
from jax import lax
from jax.sharding import PartitionSpec as P

REACH = 2


HI = lax.Precision.HIGHEST


def padded_2(cells, sides, width):
    for axis, dim in sides:
        count = lax.axis_size(axis)
        ends = count - 1
        head = lax.slice_in_dim(cells, 0, width, axis=dim)
        tail = lax.slice_in_dim(cells, cells.shape[dim] - width, cells.shape[dim], axis=dim)
        cells = jnp.concatenate(
            [
                lax.ppermute(tail, axis, [(i, (i + 1) % count) for i in range(ends)]),
                cells,
                lax.ppermute(head, axis, [((i + 1) % count, i) for i in range(ends)]),
            ],
            axis=dim,
        )
    return cells


def from_partner(x, axis, bit):
    return lax.ppermute(x, axis, [(i, i ^ 1 << bit) for i in range(lax.axis_size(axis))])


def partner_piece(state, row):
    return (state, row)


def mixed_pair(own, across_partners, factor):
    widened = factor.astype(jnp.float32)
    first = jnp.einsum("bvk,bkj->bvj", own, widened[:, 0], precision=HI)
    second = jnp.einsum("bvk,bkj->bvj", across_partners, widened[:, 1], precision=HI)
    return first + second


def on_device(
    points,
    tree_order,
    nearby_dense_blocks,
    neighbours,
    compress,
    expand,
    top_factor,
    butterfly_mixers,
    block_map,
):
    vectors = points.shape[0]
    count_pts = points.shape[1]
    leaf = nearby_dense_blocks.shape[2]
    leaves = count_pts // leaf
    near_count = neighbours.shape[1]
    device = lax.axis_index("partner") * lax.axis_size("block") + lax.axis_index("block")
    local_order = tree_order - device * count_pts
    ordered = jnp.take(points, local_order, axis=1)
    padded = padded_2(ordered, (("block", 1),), REACH * leaf)
    windows = padded.reshape(vectors, leaves + 2 * REACH, leaf)
    slots = neighbours - device * leaves + REACH
    source_points = jnp.take(windows, slots.reshape(-1), axis=1).reshape(
        vectors, leaves, near_count, leaf
    )
    nearby_field_sum = jnp.einsum(
        "zxqc,xqcf->zxf", source_points, nearby_dense_blocks, preferred_element_type=jnp.float32
    )
    leaf_rows = ordered.reshape(vectors, leaves, leaf)
    state = jnp.einsum("vbs,bsk->bvk", leaf_rows, compress, preferred_element_type=jnp.float32)
    levels = lax.axis_size("partner").bit_length() - 1
    sent, row = partner_piece(state, block_map[0])
    received = from_partner(sent, "partner", levels - 1)
    across_partners = jnp.take(received, row, axis=0)
    state = jnp.einsum(
        "bvk,bkj->bvj", across_partners, top_factor.astype(jnp.float32), precision=HI
    )
    for section in range(levels - 1):
        bit = levels - 2 - section
        sent, row = partner_piece(state, block_map[section + 1])
        received = from_partner(sent, "partner", bit)
        across_partners = jnp.take(received, row, axis=0)
        state = mixed_pair(state, across_partners, butterfly_mixers[section])
    far_field = jnp.einsum("bvk,bks->vbs", state, expand.astype(jnp.float32), precision=HI)
    in_tree = (nearby_field_sum + far_field).reshape(vectors, count_pts).astype(jnp.bfloat16)
    return jnp.zeros_like(points).at[:, local_order].set(in_tree)


def solution(mesh):
    return jax.shard_map(
        on_device,
        mesh=mesh,
        in_specs=(
            P(None, ("partner", "block")),
            P(("partner", "block")),
            P(("partner", "block"), None, None, None),
            P(("partner", "block"), None),
            P(("partner", "block"), None, None),
            P(("partner", "block"), None, None),
            P(("partner", "block"), None, None),
            P(None, ("partner", "block"), None, None, None),
            P(),
        ),
        out_specs=P(None, ("partner", "block")),
        check_vma=False,
    )
```

profile of v0, /device:TPU:1, one launch (start us, length us, event | category | flops | bytes accessed | tf_op | source)
XLA Modules:
  0.0 71.8 jit_solution(17618367198242215510)
XLA Ops:
  0.0 0.0 copy-start
  0.0 0.0 copy-start.1
  0.0 1.2 %copy.44 = bf16[32,1024]{0,1:T(8,128)(2,1)S(1)} copy(bf16[32,1024]{1,0:T(8,128)(2,1)} %param.11) | data formatting | bytes 131072 | tf_op args[0]
  1.2 0.7 compare_and_fusion
  1.9 3.2 %gather_fusion = bf16[1024,32]{1,0:T(8,128)(2,1)S(1)} fusion(bf16[32,1024]{0,1:T(8,128)(2,1)S(1)} %copy.44, s32[1024]{0:T(1024)S(1)} %broadcast_clamp_fusion), kind=kCustom, calls=%fused_computation.5 | custom fusion | bytes 135168 | tf_op jit(solution)/shard_map/jit(_take)/gather | solution.py:62
  5.1 0.2 bitcast_select_fusion
  5.3 0.0 copy-start.4
  5.3 0.7 copy-done.4
  6.0 0.6 fusion.40
  6.7 1.3 %collective-permute-start.1 = (bf16[32,256]{0,1:T(8,128)(2,1)}, bf16[32,256]{0,1:T(8,128)(2,1)}, u32[]{:S(2)}, u32[]{:S(2)}) collective-permute-start(bf16[32,256]{0,1:T(8,128)(2,1)} %get-tuple-element.23), channel_id=1, source_target_pairs={{1,0},{2,1},{3,2},{4,3},{5,4},{6,5},{7,6},{8,7},{9,8},{10,9},{11,1... | collective-permute-start | bytes 49160 | tf_op jit(solution)/shard_map/ppermute | solution.py:22
  8.0 5.6 %collective-permute-start = (bf16[32,256]{0,1:T(8,128)(2,1)}, bf16[32,256]{0,1:T(8,128)(2,1)}, u32[]{:S(2)}, u32[]{:S(2)}) collective-permute-start(bf16[32,256]{0,1:T(8,128)(2,1)} %get-tuple-element.22), channel_id=1, source_target_pairs={{0,1},{1,2},{2,3},{3,4},{4,5},{5,6},{6,7},{7,8},{8,9},{9,10},{10,1... | collective-permute-start | bytes 49160 | tf_op jit(solution)/shard_map/ppermute | solution.py:20
  13.6 0.1 copy.50
  13.7 1.8 %fusion.22 = f32[8,32,128]{2,1,0:T(8,128)} fusion(bf16[8,128,128]{2,1,0:T(8,128)(2,1)} %param.15, bf16[32,8,128]{2,0,1:T(8,128)(2,1)S(1)} %copy.50, pred[8,128]{1,0:T(8,128)(4,1)S(1)} %bitcast.98), kind=kOutput, calls=%fused_computation.52 | convolution fusion | flops 8421376 | bytes 459776 | tf_op jit(solution)/shard_map/vbs,bsk->bvk/dot_general | solution.py:73
  15.5 4.8 %collective-permute-start.2 = (f32[8,32,128]{2,1,0:T(8,128)}, f32[8,32,128]{2,1,0:T(8,128)}, u32[]{:S(2)}, u32[]{:S(2)}) collective-permute-start(f32[8,32,128]{2,1,0:T(8,128)} %fusion.22), channel_id=1, source_target_pairs={{0,256},{16,272},{32,288},{48,304},{64,320},{80,336},{96,352},{112... | collective-permute-start | bytes 393224 | tf_op jit(solution)/shard_map/ppermute | solution.py:30
  20.3 0.0 copy-done.6
  20.4 0.1 copy.48
  20.4 0.1 reshape.62
  20.5 0.6 pad_clamp_fusion.5
  21.1 0.0 copy-done.11
  21.1 0.6 compare_and_fusion.1
  21.7 0.6 pad_clamp_fusion.4
  22.3 0.0 copy-done.1
  22.3 1.4 %fusion.39 = (bf16[1,8,2,128,128]{4,3,2,1,0:T(8,128)(2,1)}, bf16[1,8,2,128,128]{4,3,2,1,0:T(8,128)(2,1)}, bf16[1,8,2,128,128]{4,3,2,1,0:T(8,128)(2,1)}, bf16[1,8,2,128,128]{4,3,2,1,0:T(8,128)(2,1)}) fusion(bf16[4,8,2,128,128]{4,3,2,1,0:T(8,128)(2,1)S(1)} %copy-done.1), kind=kLoop, calls=%fused_computation.92 | loop fusion | bytes 4194304 | tf_op jit(solution)/shard_map/slice | solution.py:86
  23.7 0.6 pad_clamp_fusion.3
  24.3 1.1 %copy.46 = bf16[32,1024]{1,0:T(8,128)(2,1)S(1)} copy(bf16[32,1024]{0,1:T(8,128)(2,1)} %copy-done.4) | data formatting | bytes 131072 | tf_op jit(solution)/shard_map/jit(_take)/select_n | solution.py:62
  25.4 0.7 copy.43
  26.1 1.1 %copy.74 = bf16[1,8,2,128,128]{4,3,1,2,0:T(8,128)(2,1)S(1)} copy(bf16[1,8,2,128,128]{4,3,2,1,0:T(8,128)(2,1)} %get-tuple-element.21) | data formatting | bytes 1048576
  27.1 1.1 %copy.73 = bf16[1,8,2,128,128]{4,3,1,2,0:T(8,128)(2,1)S(1)} copy(bf16[1,8,2,128,128]{4,3,2,1,0:T(8,128)(2,1)} %get-tuple-element.20) | data formatting | bytes 1048576
  28.2 0.0 copy-done.3
  28.3 0.0 collective-permute-done.1
  28.4 0.9 %copy.47 = bf16[32,256]{1,0:T(8,128)(2,1)S(1)} copy(bf16[32,256]{0,1:T(8,128)(2,1)} %collective-permute-done.1) | data formatting | bytes 32768 | tf_op jit(solution)/shard_map/ppermute | solution.py:22
  29.3 0.0 collective-permute-done
  29.3 0.9 %copy.45 = bf16[32,256]{1,0:T(8,128)(2,1)S(1)} copy(bf16[32,256]{0,1:T(8,128)(2,1)} %collective-permute-done) | data formatting | bytes 32768 | tf_op jit(solution)/shard_map/ppermute | solution.py:20
  30.2 0.7 gather_fusion.1
  31.0 1.0 %convolution_bitcast_fusion = f32[8,32,128]{2,1,0:T(8,128)S(1)} fusion(bf16[8,3,128,128]{3,2,1,0:T(8,128)(2,1)S(1)} %copy-done, bf16[32,8,3,128]{3,0,2,1:T(8,128)(2,1)S(1)} %bitcast.96, pred[8,3]{1,0:T(8,128)(4,1)} %copy.43), kind=kOutput, calls=%fused_computation.13 | convolution fusion | flops 25264128 | bytes 1114136 | tf_op jit(solution)/shard_map/zxqc,xqcf->zxf/dot_general | solution.py:69
  31.9 0.0 collective-permute-done.2
  31.9 1.6 %gather_fusion.2 = f32[8,32,128]{2,1,0:T(8,128)S(1)} fusion(f32[8,32,128]{2,1,0:T(8,128)} %collective-permute-done.2, s32[1024]{0:T(1024)} %pad_clamp_fusion.4), kind=kCustom, calls=%fused_computation.clone | custom fusion | bytes 262176 | tf_op jit(solution)/shard_map/jit(_take)/gather | solution.py:77
  33.5 1.3 %fusion.12 = f32[8,32,128]{2,1,0:T(8,128)S(1)} fusion(bf16[8,128,128]{2,1,0:T(8,128)(2,1)} %param.17, f32[8,32,128]{2,1,0:T(8,128)S(1)} %gather_fusion.2, pred[8]{0:T(512)(128)(4,1)} %get-tuple-element.28), kind=kOutput, calls=%fused_computation.39 | convolution fusion | flops 50364416 | bytes 524296 | tf_op jit(solution)/shard_map/bvk,bkj->bvj/dot_general | solution.py:78
  34.9 2.3 %collective-permute-start.3 = (f32[8,32,128]{2,1,0:T(8,128)S(1)}, f32[8,32,128]{2,1,0:T(8,128)S(1)}, u32[]{:S(2)}, u32[]{:S(2)}) collective-permute-start(f32[8,32,128]{2,1,0:T(8,128)S(1)} %fusion.12), channel_id=1, source_target_pairs={{0,128},{16,144},{32,160},{48,176},{64,192},{80,208},{96,224},{112... | collective-permute-start | bytes 393224 | tf_op jit(solution)/shard_map/ppermute | solution.py:30
  37.2 0.3 fusion.5
  37.5 3.1 %collective-permute-done.3 = f32[8,32,128]{2,1,0:T(8,128)S(1)} collective-permute-done((f32[8,32,128]{2,1,0:T(8,128)S(1)}, f32[8,32,128]{2,1,0:T(8,128)S(1)}, u32[]{:S(2)}, u32[]{:S(2)}) %collective-permute-start.3) | collective-permute-done | bytes 131104 | tf_op jit(solution)/shard_map/ppermute | solution.py:30
  40.6 0.7 gather_fusion.3
  41.3 0.4 convolution_add_fusion.4
  41.7 4.7 %collective-permute-start.4 = (f32[8,32,128]{2,1,0:T(8,128)S(1)}, f32[8,32,128]{2,1,0:T(8,128)S(1)}, u32[]{:S(2)}, u32[]{:S(2)}) collective-permute-start(f32[8,32,128]{2,1,0:T(8,128)S(1)} %convolution_add_fusion.4), channel_id=1, source_target_pairs={{0,64},{16,80},{32,96},{48,112},{64,0},{80,16},{96,32},{112,48},{1... | collective-permute-start | bytes 393224 | tf_op jit(solution)/shard_map/ppermute | solution.py:30
  46.3 0.0 copy-start.5
  46.3 0.3 fusion.4
  46.7 2.2 %collective-permute-done.4 = f32[8,32,128]{2,1,0:T(8,128)S(1)} collective-permute-done((f32[8,32,128]{2,1,0:T(8,128)S(1)}, f32[8,32,128]{2,1,0:T(8,128)S(1)}, u32[]{:S(2)}, u32[]{:S(2)}) %collective-permute-start.4) | collective-permute-done | bytes 131104 | tf_op jit(solution)/shard_map/ppermute | solution.py:30
  48.9 0.6 gather_fusion.4
  49.5 0.0 copy-done.9
  49.5 0.4 convolution_add_fusion.3
  49.8 3.1 %collective-permute-start.5 = (f32[8,32,128]{2,1,0:T(8,128)S(1)}, f32[8,32,128]{2,1,0:T(8,128)S(1)}, u32[]{:S(2)}, u32[]{:S(2)}) collective-permute-start(f32[8,32,128]{2,1,0:T(8,128)S(1)} %convolution_add_fusion.3), channel_id=1, source_target_pairs={{0,32},{16,48},{32,0},{48,16},{64,96},{80,112},{96,64},{112,80},{1... | collective-permute-start | bytes 393224 | tf_op jit(solution)/shard_map/ppermute | solution.py:30
  53.0 0.3 fusion.3
  53.3 2.3 %collective-permute-done.5 = f32[8,32,128]{2,1,0:T(8,128)S(1)} collective-permute-done((f32[8,32,128]{2,1,0:T(8,128)S(1)}, f32[8,32,128]{2,1,0:T(8,128)S(1)}, u32[]{:S(2)}, u32[]{:S(2)}) %collective-permute-start.5) | collective-permute-done | bytes 131104 | tf_op jit(solution)/shard_map/ppermute | solution.py:30
  55.6 0.6 gather_fusion.5
  56.1 0.4 convolution_add_fusion.2
  56.5 8.9 %collective-permute-start.6 = (f32[8,32,128]{2,1,0:T(8,128)S(1)}, f32[8,32,128]{2,1,0:T(8,128)S(1)}, u32[]{:S(2)}, u32[]{:S(2)}) collective-permute-start(f32[8,32,128]{2,1,0:T(8,128)S(1)} %convolution_add_fusion.2), channel_id=1, source_target_pairs={{0,16},{16,0},{32,48},{48,32},{64,80},{80,64},{96,112},{112,96},{1... | collective-permute-start | bytes 393224 | tf_op jit(solution)/shard_map/ppermute | solution.py:30
  65.4 0.3 fusion.2
  65.7 0.6 collective-permute-done.6
  66.4 0.6 gather_fusion.6
  66.9 0.4 convolution_add_fusion.1
  67.3 0.3 fusion.1
  67.7 0.2 copy.56
  67.8 3.2 %scatter_custom_fusion = bf16[32,1024]{0,1:T(8,128)(2,1)S(1)} fusion(s32[1024]{0:T(1024)S(1)} %get-tuple-element.17, bf16[1024,32]{1,0:T(8,128)(2,1)S(1)} %copy.56, bf16[]{:T(256)} %constant.26.clone.1), kind=kCustom, calls=%fused_computation.41 | custom fusion | bytes 65538 | tf_op jit(solution)/shard_map/scatter | solution.py:89
  71.1 0.8 %copy.57 = bf16[32,1024]{1,0:T(8,128)(2,1)} copy(bf16[32,1024]{0,1:T(8,128)(2,1)S(1)} %scatter_custom_fusion) | data formatting | bytes 131072 | tf_op jit(solution)/shard_map/scatter | solution.py:89
  (25 shorter events, 0.2 us)
Async XLA Ops:
  0.0 30.9 %copy-start = (bf16[8,3,128,128]{3,2,1,0:T(8,128)(2,1)S(1)}, bf16[8,3,128,128]{3,2,1,0:T(8,128)(2,1)}, u32[]{:S(2)}) copy-start(bf16[8,3,128,128]{3,2,1,0:T(8,128)(2,1)} %param.13) | copy-start | bytes 2359300
  0.0 20.3 %copy-start.6 = (s32[8,3]{0,1:T(4,128)S(1)}, s32[8,3]{0,1:T(4,128)}, u32[]{:S(2)}) copy-start(s32[8,3]{0,1:T(4,128)} %param.14) | copy-start | bytes 292
  0.0 21.1 %copy-start.11 = (s32[5,8]{1,0:T(8,128)S(1)}, s32[5,8]{1,0:T(8,128)}, u32[]{:S(2)}) copy-start(s32[5,8]{1,0:T(8,128)} %param.19) | copy-start | bytes 484
  0.0 22.3 %copy-start.1 = (bf16[4,8,2,128,128]{4,3,2,1,0:T(8,128)(2,1)S(1)}, bf16[4,8,2,128,128]{4,3,2,1,0:T(8,128)(2,1)}, u32[]{:S(2)}) copy-start(bf16[4,8,2,128,128]{4,3,2,1,0:T(8,128)(2,1)} %param.18) | copy-start | bytes 6291460
  5.3 0.7 copy-start.4
  6.7 21.7 %collective-permute-start.1 = (bf16[32,256]{0,1:T(8,128)(2,1)}, bf16[32,256]{0,1:T(8,128)(2,1)}, u32[]{:S(2)}, u32[]{:S(2)}) collective-permute-start(bf16[32,256]{0,1:T(8,128)(2,1)} %get-tuple-element.23), channel_id=1, source_target_pairs={{1,0},{2,1},{3,2},{4,3},{5,4},{6,5},{7,6},{8,7},{9,8},{10,9},{11,1... | collective-permute-start | bytes 49160 | tf_op jit(solution)/shard_map/ppermute | solution.py:22
  8.0 21.3 %collective-permute-start = (bf16[32,256]{0,1:T(8,128)(2,1)}, bf16[32,256]{0,1:T(8,128)(2,1)}, u32[]{:S(2)}, u32[]{:S(2)}) collective-permute-start(bf16[32,256]{0,1:T(8,128)(2,1)} %get-tuple-element.22), channel_id=1, source_target_pairs={{0,1},{1,2},{2,3},{3,4},{4,5},{5,6},{6,7},{7,8},{8,9},{9,10},{10,1... | collective-permute-start | bytes 49160 | tf_op jit(solution)/shard_map/ppermute | solution.py:20
  15.5 16.4 %collective-permute-start.2 = (f32[8,32,128]{2,1,0:T(8,128)}, f32[8,32,128]{2,1,0:T(8,128)}, u32[]{:S(2)}, u32[]{:S(2)}) collective-permute-start(f32[8,32,128]{2,1,0:T(8,128)} %fusion.22), channel_id=1, source_target_pairs={{0,256},{16,272},{32,288},{48,304},{64,320},{80,336},{96,352},{112... | collective-permute-start | bytes 393224 | tf_op jit(solution)/shard_map/ppermute | solution.py:30
  23.7 4.5 %copy-start.3 = (bf16[1,8,2,128,128]{4,3,2,1,0:T(8,128)(2,1)S(1)}, bf16[1,8,2,128,128]{4,3,2,1,0:T(8,128)(2,1)}, u32[]{:S(2)}) copy-start(bf16[1,8,2,128,128]{4,3,2,1,0:T(8,128)(2,1)} %get-tuple-element.19) | copy-start | bytes 1572868
  23.7 4.6 %copy-start.2 = (bf16[1,8,2,128,128]{4,3,2,1,0:T(8,128)(2,1)S(1)}, bf16[1,8,2,128,128]{4,3,2,1,0:T(8,128)(2,1)}, u32[]{:S(2)}) copy-start(bf16[1,8,2,128,128]{4,3,2,1,0:T(8,128)(2,1)} %get-tuple-element.18) | copy-start | bytes 1572868
  28.3 12.9 %copy-start.10 = (pred[8]{0:T(512)(128)(4,1)S(1)}, pred[8]{0:T(512)(128)(4,1)}, u32[]{:S(2)}) copy-start(pred[8]{0:T(512)(128)(4,1)} %get-tuple-element.26) | copy-start | bytes 28
  30.9 18.5 %copy-start.9 = (pred[8]{0:T(512)(128)(4,1)S(1)}, pred[8]{0:T(512)(128)(4,1)}, u32[]{:S(2)}) copy-start(pred[8]{0:T(512)(128)(4,1)} %get-tuple-element.24) | copy-start | bytes 28
  33.5 22.6 %copy-start.8 = (pred[8]{0:T(512)(128)(4,1)S(1)}, pred[8]{0:T(512)(128)(4,1)}, u32[]{:S(2)}) copy-start(pred[8]{0:T(512)(128)(4,1)} %get-tuple-element.30) | copy-start | bytes 28
  34.9 5.7 %collective-permute-start.3 = (f32[8,32,128]{2,1,0:T(8,128)S(1)}, f32[8,32,128]{2,1,0:T(8,128)S(1)}, u32[]{:S(2)}, u32[]{:S(2)}) collective-permute-start(f32[8,32,128]{2,1,0:T(8,128)S(1)} %fusion.12), channel_id=1, source_target_pairs={{0,128},{16,144},{32,160},{48,176},{64,192},{80,208},{96,224},{112... | collective-permute-start | bytes 393224 | tf_op jit(solution)/shard_map/ppermute | solution.py:30
  41.3 25.6 %copy-start.7 = (pred[8]{0:T(512)(128)(4,1)S(1)}, pred[8]{0:T(512)(128)(4,1)}, u32[]{:S(2)}) copy-start(pred[8]{0:T(512)(128)(4,1)} %get-tuple-element.6) | copy-start | bytes 28
  41.7 7.2 %collective-permute-start.4 = (f32[8,32,128]{2,1,0:T(8,128)S(1)}, f32[8,32,128]{2,1,0:T(8,128)S(1)}, u32[]{:S(2)}, u32[]{:S(2)}) collective-permute-start(f32[8,32,128]{2,1,0:T(8,128)S(1)} %convolution_add_fusion.4), channel_id=1, source_target_pairs={{0,64},{16,80},{32,96},{48,112},{64,0},{80,16},{96,32},{112,48},{1... | collective-permute-start | bytes 393224 | tf_op jit(solution)/shard_map/ppermute | solution.py:30
  46.3 21.0 %copy-start.5 = (bf16[8,128,128]{2,1,0:T(8,128)(2,1)S(1)}, bf16[8,128,128]{2,1,0:T(8,128)(2,1)}, u32[]{:S(2)}) copy-start(bf16[8,128,128]{2,1,0:T(8,128)(2,1)} %param.16) | copy-start | bytes 786436
  49.8 5.7 %collective-permute-start.5 = (f32[8,32,128]{2,1,0:T(8,128)S(1)}, f32[8,32,128]{2,1,0:T(8,128)S(1)}, u32[]{:S(2)}, u32[]{:S(2)}) collective-permute-start(f32[8,32,128]{2,1,0:T(8,128)S(1)} %convolution_add_fusion.3), channel_id=1, source_target_pairs={{0,32},{16,48},{32,0},{48,16},{64,96},{80,112},{96,64},{112,80},{1... | collective-permute-start | bytes 393224 | tf_op jit(solution)/shard_map/ppermute | solution.py:30
  56.5 9.8 %collective-permute-start.6 = (f32[8,32,128]{2,1,0:T(8,128)S(1)}, f32[8,32,128]{2,1,0:T(8,128)S(1)}, u32[]{:S(2)}, u32[]{:S(2)}) collective-permute-start(f32[8,32,128]{2,1,0:T(8,128)S(1)} %convolution_add_fusion.2), channel_id=1, source_target_pairs={{0,16},{16,0},{32,48},{48,32},{64,80},{80,64},{96,112},{112,96},{1... | collective-permute-start | bytes 393224 | tf_op jit(solution)/shard_map/ppermute | solution.py:30
where the time goes:
time: 72.4 us; the launch traced here: 71.8 us
  starting transfers between devices  30.7 us (42%)
  local copies, waits for them, and re-layouts  21.9 us (30%)
  waiting for transfers between devices  8.24 us (11%)
  matrix products  7.16 us (10%)
  other arithmetic  3.37 us (5%)
    ppermute x5, starting transfers between devices, from_partner(): lax.ppermute(x, axis, [(i, i ^ 1 << bit) for i in range(lax.axis_size(axi...  23.8 us
    ppermute x5, waiting for transfers between devices, from_partner(): lax.ppermute(x, axis, [(i, i ^ 1 << bit) for i in range(lax.axis_size(axi...  8.22 us
    ppermute x1, starting transfers between devices, padded_2(): lax.ppermute(tail, axis, [(i, (i + 1) % count) for i in range(ends)])  5.62 us
    unnamed x29, local copies, waits for them, and re-layouts  4.13 us
    scatter x2, local copies, waits for them, and re-layouts, on_device(): return jnp.zeros_like(points).at[:, local_order].set(in_tree)  3.98 us
    gather x5, local copies, waits for them, and re-layouts, on_device(): across_partners = jnp.take(received, row, axis=0)  3.92 us
    gather x2, local copies, waits for them, and re-layouts, on_device(): ordered = jnp.take(points, local_order, axis=1)  3.33 us
    dot_general x1, matrix products, on_device(): jnp.einsum('vbs,bsk->bvk', leaf_rows, compress, preferred_element_type=jn...  1.79 us
  transfers between devices with their start and end apart: 7, of which 4 were waited for; matrix products, arithmetic and copies ran while one was open for 20% of the time, Pallas kernels for 0%

commit v1 on v0

v1 whole, which is shorter than its diff:
```python
import functools

import jax
import jax.numpy as jnp
from jax import lax
from jax.experimental import pallas as pl
from jax.experimental.pallas import tpu as pltpu
from jax.sharding import PartitionSpec as P

BF = jnp.bfloat16
F32 = jnp.float32
MESH = pl.DeviceIdType.MESH
LEAVES = 8
LEAF = 128
NV = 32
SENT = 4


def dot(a, b):
    return jnp.dot(a, b, preferred_element_type=F32)


def halves(x):
    high = x.astype(BF)
    return high, (x - high.astype(F32)).astype(BF)


def stacked(x):
    return jnp.concatenate(halves(x), axis=0)


def paired(w):
    return jnp.concatenate(halves(w), axis=1)


def apply_factor(x, w):
    y = dot(x, w)
    return (y[:NV, :LEAF] + y[NV:, :LEAF]) + y[:NV, LEAF:]


def lane_gather(chunks, where, lane):
    lanes = jnp.broadcast_to(lane, (NV, LEAF))
    chunk_of = jnp.broadcast_to(where, (NV, LEAF))
    out = None
    for k, chunk in enumerate(chunks):
        picked = jnp.take_along_axis(chunk, lanes, axis=1, mode="promise_in_bounds")
        out = picked if out is None else jnp.where(chunk_of == k, picked, out)
    return out


def level_tables(values):
    mask = functools.reduce(lambda a, b: a | b, [jnp.int32(1) << v for v in values])
    chosen = []
    for _ in range(SENT):
        low = mask & (-mask)
        mask = mask ^ low
        chosen.append(sum((low >= (1 << c)).astype(jnp.int32) for c in range(1, LEAVES)))
    places = [sum((c < v).astype(jnp.int32) for c in chosen[:-1]) for v in values]
    return chosen, places


def kernel(
    points, order, near, neighbours, compress, expand, top, mixers, block_map,
    out_ref,
    pts_v, ord_v, near_v, com_v, exp_v, top_v, mix_v, near_s, map_s, tab_s,
    win, field, inv_w, inv_l, acc, out_v,
    snd1, r16, r24, top8_s, top8_r, mix2_s, mix2_r,
    snd2a, snd2b, r4, r6, r2, snd3, r1,
    w1, w2, w3, st2, st4,
    load_sem, ssem, rsem,
):
    p = lax.axis_index("partner")
    b = lax.axis_index("block")
    n_b = lax.axis_size("block")
    me = p * n_b + b
    right = lax.rem(b + 1, n_b)
    left = lax.rem(b + n_b - 1, n_b)

    barrier = pltpu.get_barrier_semaphore()
    for m in (16, 24, 8, 4, 6, 2, 1):
        pl.semaphore_signal(barrier, inc=1, device_id=(p ^ m, b), device_id_type=MESH)
    for z in (left, right):
        pl.semaphore_signal(barrier, inc=1, device_id=(p, z), device_id_type=MESH)

    loads = {}
    for k, (name, src, dst) in enumerate((
        ("map", block_map, map_s), ("order", order, ord_v), ("points", points, pts_v), ("compress", compress, com_v),
        ("top", top, top_v), ("mixers", mixers, mix_v), ("neighbours", neighbours, near_s), ("near", near, near_v),
        ("expand", expand, exp_v),
    )):
        loads[name] = pltpu.make_async_copy(src, dst, load_sem.at[k])
        loads[name].start()

    used = [0]
    sends = []

    def send(src, dst, to):
        k = used[0]
        used[0] += 1
        c = pltpu.make_async_remote_copy(
            src_ref=src, dst_ref=dst, send_sem=ssem.at[k], recv_sem=rsem.at[k], device_id=to, device_id_type=MESH
        )
        c.start()
        sends.append(c)
        return c

    loads["map"].wait()
    chosen, places, entries = [], [], []
    for j in range(5):
        row = [map_s[j, i] for i in range(LEAVES)]
        c, q = level_tables(row)
        chosen.append(c)
        places.append(q)
        entries.append(row)
        for i in range(LEAVES):
            tab_s[j, i] = q[i]

    loads["order"].wait()
    local = ord_v[...] - me * (LEAVES * LEAF)
    ord_v[...] = local
    loads["points"].wait()
    chunks = [pts_v[:, pl.ds(k * LEAF, LEAF)].astype(F32) for k in range(LEAVES)]
    loads["compress"].wait()
    pl.semaphore_wait(barrier, 9)
    first = []
    for s in range(SENT):
        c = chosen[0][s]
        row = ord_v[pl.ds(c, 1), :]
        rows = lane_gather(chunks, row >> 7, row & 127).astype(BF)
        snd1[s] = stacked(dot(rows, com_v[c]))
        first.append(send(snd1.at[s], r16.at[s], (p ^ 16, b)))
        first.append(send(snd1.at[s], r24.at[s], (p ^ 24, b)))

    loads["top"].wait()
    for s in range(SENT):
        top8_s[s] = top_v[chosen[1][s]]
    top_copy = send(top8_s, top8_r, (p ^ 8, b))
    for l in range(LEAVES):
        row = ord_v[pl.ds(l, 1), :]
        win[l + 2] = lane_gather(chunks, row >> 7, row & 127).astype(BF)
    halo_right = send(win.at[pl.ds(LEAVES, 2)], win.at[pl.ds(0, 2)], (p, right))
    halo_left = send(win.at[pl.ds(2, 2)], win.at[pl.ds(LEAVES + 2, 2)], (p, left))
    loads["mixers"].wait()
    for s in range(SENT):
        mix2_s[s] = mix_v[1, chosen[3][s]]
    mix_copy = send(mix2_s, mix2_r, (p ^ 2, b))

    for i in range(LEAVES):
        w1[i, pl.ds(0, LEAF)] = paired(dot(top_v[i], mix_v[0, i, 0]))
    top_copy.wait_recv()
    for i in range(LEAVES):
        w1[i, pl.ds(LEAF, LEAF)] = paired(dot(top8_r[places[1][i]], mix_v[0, i, 1]))

    for c in first:
        c.wait_recv()

    def skeleton_2(c):
        own = r16[tab_s[0, c]]
        other = r24[tab_s[0, map_s[1, c]]]
        return apply_factor(jnp.concatenate([own, other], axis=1), w1[c])

    second = []
    for s in range(SENT):
        snd2a[s] = stacked(skeleton_2(chosen[2][s]))
        second.append(send(snd2a.at[s], r4.at[s], (p ^ 4, b)))
        second.append(send(snd2a.at[s], r6.at[s], (p ^ 6, b)))
    for s in range(SENT):
        snd2b[s] = stacked(skeleton_2(chosen[3][s]))
        second.append(send(snd2b.at[s], r2.at[s], (p ^ 2, b)))
    for i in range(LEAVES):
        st2[i] = stacked(skeleton_2(i))

    for i in range(LEAVES):
        own = mix_v[1, i].reshape(2 * LEAF, LEAF)
        w2[i, pl.ds(0, 2 * LEAF)] = paired(dot(own, mix_v[2, i, 0]))
        acc[i] = apply_factor(st2[i], w2[i, pl.ds(0, LEAF)])
    mix_copy.wait_recv()
    for i in range(LEAVES):
        other = mix2_r[places[3][i]].reshape(2 * LEAF, LEAF)
        w2[i, pl.ds(2 * LEAF, 2 * LEAF)] = paired(dot(other, mix_v[2, i, 1]))
    loads["expand"].wait()
    for i in range(LEAVES):
        w3[i] = paired(dot(mix_v[3, i].reshape(2 * LEAF, LEAF), exp_v[i]))
    loads["near"].wait()
    loads["neighbours"].wait()
    halo_right.wait_recv()
    halo_left.wait_recv()
    for i in range(LEAVES):
        rows = jnp.concatenate([win[jnp.clip(near_s[n, i] - me * LEAVES + 2, 0, LEAVES + 3)] for n in range(3)], axis=1)
        field[i] = dot(rows, near_v[i].reshape(3 * LEAF, LEAF))
    sub = lax.broadcasted_iota(jnp.int32, (LEAVES, LEAF), 0)
    lane = lax.broadcasted_iota(jnp.int32, (LEAVES, LEAF), 1)
    tall = lax.broadcasted_iota(jnp.int32, (LEAF, LEAF), 0)
    table = jnp.zeros((2 * LEAVES, LEAF), F32)
    for l in range(LEAVES):
        row = ord_v[pl.ds(l, 1), :]
        here = jnp.broadcast_to(row >> 7, (LEAVES, LEAF)) == sub
        digits = jnp.concatenate(
            [jnp.where(here, float(l), 0.0), jnp.where(here, lane.astype(F32), 0.0)], axis=0
        ).astype(BF)
        spots = jnp.where(jnp.broadcast_to(row & 127, (LEAF, LEAF)) == tall, 1.0, 0.0).astype(BF)
        table += lax.dot_general(digits, spots, (((1,), (1,)), ((), ())), preferred_element_type=F32)
    inv_w[...] = table[:LEAVES].astype(jnp.int32)
    inv_l[...] = table[LEAVES:].astype(jnp.int32)

    for c in second:
        c.wait_recv()

    def skeleton_4(c):
        x = jnp.concatenate([r4[tab_s[2, c]], r2[tab_s[3, c]], r6[tab_s[2, map_s[3, c]]]], axis=1)
        return acc[c] + apply_factor(x, w2[c, pl.ds(LEAF, 3 * LEAF)])

    third = []
    for s in range(SENT):
        snd3[s] = stacked(skeleton_4(chosen[4][s]))
        third.append(send(snd3.at[s], r1.at[s], (p ^ 1, b)))
    for i in range(LEAVES):
        st4[i] = stacked(skeleton_4(i))
    for i in range(LEAVES):
        field[i] = field[i] + apply_factor(st4[i], w3[i, pl.ds(0, LEAF)])
    for c in third:
        c.wait_recv()
    tree = []
    for i in range(LEAVES):
        tree.append(field[i] + apply_factor(r1[places[4][i]], w3[i, pl.ds(LEAF, LEAF)]))
    for l in range(LEAVES):
        out_v[:, pl.ds(l * LEAF, LEAF)] = lane_gather(tree, inv_w[pl.ds(l, 1), :], inv_l[pl.ds(l, 1), :]).astype(BF)
    done = pltpu.make_async_copy(out_v, out_ref, load_sem.at[9])
    done.start()
    for c in sends:
        c.wait_send()
    done.wait()


def on_device(points, tree_order, near, neighbours, compress, expand, top, mixers, block_map):
    skeleton = pltpu.VMEM((SENT, 2 * NV, LEAF), BF)
    n_copies = 8 + 4 + 12 + 4
    return pl.pallas_call(
        kernel,
        out_shape=jax.ShapeDtypeStruct(points.shape, points.dtype),
        in_specs=[pl.BlockSpec(memory_space=pltpu.HBM)] * 9,
        out_specs=pl.BlockSpec(memory_space=pltpu.HBM),
        scratch_shapes=[
            pltpu.VMEM(points.shape, BF), pltpu.VMEM((LEAVES, LEAF), jnp.int32), pltpu.VMEM(near.shape, BF),
            pltpu.VMEM(compress.shape, BF), pltpu.VMEM(expand.shape, BF), pltpu.VMEM(top.shape, BF),
            pltpu.VMEM(mixers.shape, BF), pltpu.SMEM(neighbours.shape[::-1], jnp.int32), pltpu.SMEM(block_map.shape, jnp.int32),
            pltpu.SMEM(block_map.shape, jnp.int32),
            pltpu.VMEM((LEAVES + 4, NV, LEAF), BF), pltpu.VMEM((LEAVES, NV, LEAF), F32),
            pltpu.VMEM((LEAVES, LEAF), jnp.int32), pltpu.VMEM((LEAVES, LEAF), jnp.int32),
            pltpu.VMEM((LEAVES, NV, LEAF), F32), pltpu.VMEM(points.shape, BF),
            skeleton, skeleton, skeleton,
            pltpu.VMEM((SENT, LEAF, LEAF), BF), pltpu.VMEM((SENT, LEAF, LEAF), BF),
            pltpu.VMEM((SENT, 2, LEAF, LEAF), BF), pltpu.VMEM((SENT, 2, LEAF, LEAF), BF),
            skeleton, skeleton, skeleton, skeleton, skeleton, skeleton, skeleton,
            pltpu.VMEM((LEAVES, 2 * LEAF, 2 * LEAF), BF), pltpu.VMEM((LEAVES, 4 * LEAF, 2 * LEAF), BF),
            pltpu.VMEM((LEAVES, 2 * LEAF, 2 * LEAF), BF),
            pltpu.VMEM((LEAVES, 2 * NV, LEAF), BF), pltpu.VMEM((LEAVES, 2 * NV, LEAF), BF),
            pltpu.SemaphoreType.DMA((10,)), pltpu.SemaphoreType.DMA((n_copies,)), pltpu.SemaphoreType.DMA((n_copies,)),
        ],
        compiler_params=pltpu.CompilerParams(collective_id=0, has_side_effects=True, vmem_limit_bytes=58 * 2**20),
        cost_estimate=pl.CostEstimate(flops=200_000_000, bytes_accessed=4_000_000, transcendentals=0),
        name="butterfly",
    )(points, tree_order.reshape(LEAVES, LEAF), near, neighbours.T, compress, expand, top, mixers, block_map)


def solution(mesh):
    both = ("partner", "block")
    return jax.shard_map(
        on_device,
        mesh=mesh,
        in_specs=(
            P(None, both),
            P(both),
            P(both, None, None, None),
            P(both, None),
            P(both, None, None),
            P(both, None, None),
            P(both, None, None),
            P(None, both, None, None, None),
            P(),
        ),
        out_specs=P(None, both),
        check_vma=False,
    )
```

time: 72.4 us -> 29.1 us (0.40)
  starting transfers between devices: 30.7 us -> 0 us
  Pallas kernels: 0 us -> 27.5 us
  local copies, waits for them, and re-layouts: 21.9 us -> 1.47 us
  waiting for transfers between devices: 8.24 us -> 0 us
  matrix products: 7.16 us -> 0 us
  other arithmetic: 3.37 us -> 0 us
    ppermute x7 -> x0, starting transfers between devices: 30.7 us -> none  [the longest x5 23.8 us: from_partner(): lax.ppermute(x, axis, [(i, i ^ 1 << bit) for i in range(lax.axis_size(axi...]
    pallas_call x0 -> x1, Pallas kernels: none -> 27.5 us  [on_device(): pl.pallas_call(kernel, out_shape=jax.ShapeDtypeStruct(points.shape, point...]
    ppermute x7 -> x0, waiting for transfers between devices: 8.24 us -> none  [the longest x5 8.22 us: from_partner(): lax.ppermute(x, axis, [(i, i ^ 1 << bit) for i in range(lax.axis_size(axi...]
    gather x8 -> x0, local copies, waits for them, and re-layouts: 7.96 us -> none  [the longest x5 3.92 us: on_device(): across_partners = jnp.take(received, row, axis=0)]
    dot_general x12 -> x0, matrix products: 7.16 us -> none  [the longest x1 1.79 us: on_device(): jnp.einsum('vbs,bsk->bvk', leaf_rows, compress, preferred_element_type=jn...]
    scatter x2 -> x0, local copies, waits for them, and re-layouts: 3.98 us -> none  [on_device(): return jnp.zeros_like(points).at[:, local_order].set(in_tree)]
    unnamed x29 -> x1, local copies, waits for them, and re-layouts: 4.13 us -> 1.47 us
    slice x2 -> x0, local copies, waits for them, and re-layouts: 2 us -> none  [the longest x1 1.36 us: on_device(): state = mixed_pair(state, across_partners, butterfly_mixers[section])]
  transfers between devices with their start and end apart: 7 -> 0, of which waited for: 4 -> 0; matrix products, arithmetic and copies ran while one was open for 20% -> 0% of each run, Pallas kernels for 0% -> 0%
where the time goes in v1:
time: 29.1 us; the launch traced here: 29 us
  Pallas kernels  27.5 us (95%)
  local copies, waits for them, and re-layouts  1.47 us (5%)
    pallas_call x1, Pallas kernels, on_device(): pl.pallas_call(kernel, out_shape=jax.ShapeDtypeStruct(points.shape, point...  27.5 us
    unnamed x1, local copies, waits for them, and re-layouts  1.47 us

profile of v1, /device:TPU:1, one launch (start us, length us, event | category | flops | bytes accessed | tf_op | source)
XLA Modules:
  0.0 29.0 jit_solution(4893210960650458811)
XLA Ops:
  0.0 27.5 %butterfly.1 = bf16[32,1024]{1,0:T(8,128)(2,1)} custom-call(bf16[32,1024]{1,0:T(8,128)(2,1)} %points.1, s32[8,128]{1,0:T(8,128)} %bitcast.2, bf16[8,3,128,128]{3,2,1,0:T(8,128)(2,1)} %near.1, s32[3,8]{1,0:T(4,128)} %bitcast.3, bf16[8,128,128]{2,1,0:T(8,128)(2,1)} %compress.1, bf16[8,128,128]{2,1,0:T(8,128)(2,1)} %expand.1, bf16[8,128,128]{2,1,0:T(8,128)(2,1)} %top.1, ...), custom_call_target="tpu_custom_call" | custom-call | flops 200000000 | bytes 4000000 | tf_op jit(solution)/shard_map/butterfly/pallas_call | solution.py:238
  27.5 1.5 %copy.11 = bf16[32,1024]{1,0:T(8,128)(2,1)} copy(bf16[32,1024]{1,0:T(8,128)(2,1)} %butterfly.1) | data formatting | bytes 131072

commit v2 on v1

v2 whole, which is shorter than its diff:
```python
import functools

import jax
import jax.numpy as jnp
from jax import lax
from jax.experimental import pallas as pl
from jax.experimental.pallas import tpu as pltpu
from jax.sharding import PartitionSpec as P

BF = jnp.bfloat16
F32 = jnp.float32
MESH = pl.DeviceIdType.MESH
LEAVES = 8
LEAF = 128
NV = 32
SENT = 4


def dot(a, b):
    return jnp.dot(a, b, preferred_element_type=F32)


def halves(x):
    high = x.astype(BF)
    return high, (x - high.astype(F32)).astype(BF)


def stacked(x):
    return jnp.concatenate(halves(x), axis=0)


def paired(w):
    return jnp.concatenate(halves(w), axis=1)


def apply_factor(x, w):
    y = dot(x, w)
    return (y[:NV, :LEAF] + y[NV:, :LEAF]) + y[:NV, LEAF:]


def lane_gather(chunks, where, lane):
    lanes = jnp.broadcast_to(lane, (NV, LEAF))
    chunk_of = jnp.broadcast_to(where, (NV, LEAF))
    out = None
    for k, chunk in enumerate(chunks):
        picked = jnp.take_along_axis(chunk, lanes, axis=1, mode="promise_in_bounds")
        out = picked if out is None else jnp.where(chunk_of == k, picked, out)
    return out


def level_tables(values):
    mask = functools.reduce(lambda a, b: a | b, [jnp.int32(1) << v for v in values])
    chosen = []
    for _ in range(SENT):
        low = mask & (-mask)
        mask = mask ^ low
        chosen.append(sum((low >= (1 << c)).astype(jnp.int32) for c in range(1, LEAVES)))
    places = [sum((c < v).astype(jnp.int32) for c in chosen[:-1]) for v in values]
    return chosen, places


def kernel(
    points, order, near, neighbours, compress, expand, top, mixers, block_map,
    out_ref,
    pts_v, ord_v, near_v, com_v, exp_v, top_v, mix_v, near_s, map_s, tab_s,
    win, field, inv_w, inv_l, acc, out_v,
    snd1, r16, r24, top8_s, top8_r, mix2_s, mix2_r,
    snd2a, snd2b, r4, r6, r2, snd3, r1,
    w1, w2, w3, st2, st4,
    load_sem, ssem, rsem, halo_ssem, halo_rsem,
):
    p = lax.axis_index("partner")
    b = lax.axis_index("block")
    n_b = lax.axis_size("block")
    me = p * n_b + b
    has_left, has_right = b > 0, b < n_b - 1
    sides = ((has_left, b - 1), (has_right, b + 1))

    barrier = pltpu.get_barrier_semaphore()
    loads = {}

    def load(k, name, src, dst):
        loads[name] = pltpu.make_async_copy(src, dst, load_sem.at[k])
        loads[name].start()

    partners = (16, 24, 8, 4, 6, 2, 1)
    load(0, "map", block_map, map_s)
    load(1, "order", order, ord_v)
    for m in partners[:3]:
        pl.semaphore_signal(barrier, inc=1, device_id=(p ^ m, b), device_id_type=MESH)
    load(2, "points", points, pts_v)
    load(3, "compress", compress, com_v)
    load(4, "top", top, top_v)
    for m in partners[3:]:
        pl.semaphore_signal(barrier, inc=1, device_id=(p ^ m, b), device_id_type=MESH)
    for there, z in sides:
        @pl.when(there)
        def _():
            pl.semaphore_signal(barrier, inc=1, device_id=(p, z), device_id_type=MESH)
    load(5, "mixers", mixers, mix_v)
    load(6, "expand", expand, exp_v)
    load(7, "near", near, near_v)
    load(8, "neighbours", neighbours, near_s)

    used = [0]
    sends = []

    def send(src, dst, to):
        k = used[0]
        used[0] += 1
        c = pltpu.make_async_remote_copy(
            src_ref=src, dst_ref=dst, send_sem=ssem.at[k], recv_sem=rsem.at[k], device_id=to, device_id_type=MESH
        )
        c.start()
        sends.append(c)
        return c

    loads["map"].wait()
    chosen, places = {}, {}

    def tables(j):
        chosen[j], places[j] = level_tables([map_s[j, i] for i in range(LEAVES)])
        for i in range(LEAVES):
            tab_s[j, i] = places[j][i]

    tables(0)
    tables(1)

    loads["order"].wait()
    loads["points"].wait()
    chunks = [pts_v[:, pl.ds(k * LEAF, LEAF)].astype(F32) for k in range(LEAVES)]
    loads["compress"].wait()
    for s in range(SENT):
        c = chosen[0][s]
        row = ord_v[pl.ds(c, 1), :]
        rows = lane_gather(chunks, (row >> 7) & 7, row & 127).astype(BF)
        snd1[s] = stacked(dot(rows, com_v[c]))
    loads["top"].wait()
    for s in range(SENT):
        top8_s[s] = top_v[chosen[1][s]]

    pl.semaphore_wait(barrier, len(partners) + has_left.astype(jnp.int32) + has_right.astype(jnp.int32))
    first = [send(snd1, r16, (p ^ 16, b)), send(snd1, r24, (p ^ 24, b))]
    top_copy = send(top8_s, top8_r, (p ^ 8, b))
    for j in range(2, 5):
        tables(j)
    for l in range(LEAVES):
        row = ord_v[pl.ds(l, 1), :]
        win[l + 2] = lane_gather(chunks, (row >> 7) & 7, row & 127).astype(BF)
    halo = []
    for k, (there, z, src, dst) in enumerate(((*sides[1], LEAVES, 0), (*sides[0], 2, LEAVES + 2))):
        copy = pltpu.make_async_remote_copy(
            src_ref=win.at[pl.ds(src, 2)], dst_ref=win.at[pl.ds(dst, 2)], send_sem=halo_ssem.at[k],
            recv_sem=halo_rsem.at[k], device_id=(p, z), device_id_type=MESH,
        )
        halo.append((there, sides[k][0], copy, dst))

        @pl.when(there)
        def _():
            copy.start()

        @pl.when(jnp.logical_not(sides[k][0]))
        def _():
            win[dst] = jnp.zeros((NV, LEAF), BF)
            win[dst + 1] = jnp.zeros((NV, LEAF), BF)
    loads["mixers"].wait()
    for s in range(SENT):
        mix2_s[s] = mix_v[1, chosen[3][s]]
    mix_copy = send(mix2_s, mix2_r, (p ^ 2, b))

    for i in range(LEAVES):
        w1[i, pl.ds(0, LEAF)] = paired(dot(top_v[i], mix_v[0, i, 0]))
    for i in range(LEAVES):
        w2[i, pl.ds(0, 2 * LEAF)] = paired(dot(mix_v[1, i].reshape(2 * LEAF, LEAF), mix_v[2, i, 0]))
    loads["expand"].wait()
    for i in range(LEAVES):
        w3[i] = paired(dot(mix_v[3, i].reshape(2 * LEAF, LEAF), exp_v[i]))
    sub = lax.broadcasted_iota(jnp.int32, (LEAVES, LEAF), 0)
    lane = lax.broadcasted_iota(jnp.int32, (LEAVES, LEAF), 1)
    tall = lax.broadcasted_iota(jnp.int32, (LEAF, LEAF), 0)
    table = jnp.zeros((2 * LEAVES, LEAF), F32)
    for l in range(LEAVES):
        row = ord_v[pl.ds(l, 1), :]
        here = jnp.broadcast_to((row >> 7) & 7, (LEAVES, LEAF)) == sub
        digits = jnp.concatenate(
            [jnp.where(here, float(l), 0.0), jnp.where(here, lane.astype(F32), 0.0)], axis=0
        ).astype(BF)
        spots = jnp.where(jnp.broadcast_to(row & 127, (LEAF, LEAF)) == tall, 1.0, 0.0).astype(BF)
        table += lax.dot_general(digits, spots, (((1,), (1,)), ((), ())), preferred_element_type=F32)
    inv_w[...] = table[:LEAVES].astype(jnp.int32)
    inv_l[...] = table[LEAVES:].astype(jnp.int32)

    top_copy.wait_recv()
    for i in range(LEAVES):
        w1[i, pl.ds(LEAF, LEAF)] = paired(dot(top8_r[places[1][i]], mix_v[0, i, 1]))

    for c in first:
        c.wait_recv()

    def skeleton_2(c):
        own = r16[tab_s[0, c]]
        other = r24[tab_s[0, map_s[1, c]]]
        return apply_factor(jnp.concatenate([own, other], axis=1), w1[c])

    for s in range(SENT):
        snd2a[s] = stacked(skeleton_2(chosen[2][s]))
    second = [send(snd2a, r4, (p ^ 4, b)), send(snd2a, r6, (p ^ 6, b))]
    for s in range(SENT):
        snd2b[s] = stacked(skeleton_2(chosen[3][s]))
    second.append(send(snd2b, r2, (p ^ 2, b)))
    for i in range(LEAVES):
        st2[i] = stacked(skeleton_2(i))

    for i in range(LEAVES):
        acc[i] = apply_factor(st2[i], w2[i, pl.ds(0, LEAF)])
    mix_copy.wait_recv()
    for i in range(LEAVES):
        other = mix2_r[places[3][i]].reshape(2 * LEAF, LEAF)
        w2[i, pl.ds(2 * LEAF, 2 * LEAF)] = paired(dot(other, mix_v[2, i, 1]))
    loads["near"].wait()
    loads["neighbours"].wait()
    for _, comes, copy, _ in halo:
        @pl.when(comes)
        def _():
            copy.wait_recv()
    for i in range(LEAVES):
        rows = jnp.concatenate([win[jnp.clip(near_s[n, i] - me * LEAVES + 2, 0, LEAVES + 3)] for n in range(3)], axis=1)
        field[i] = dot(rows, near_v[i].reshape(3 * LEAF, LEAF))
    for c in second:
        c.wait_recv()

    def skeleton_4(c):
        x = jnp.concatenate([r4[tab_s[2, c]], r2[tab_s[3, c]], r6[tab_s[2, map_s[3, c]]]], axis=1)
        return acc[c] + apply_factor(x, w2[c, pl.ds(LEAF, 3 * LEAF)])

    for s in range(SENT):
        snd3[s] = stacked(skeleton_4(chosen[4][s]))
    third = send(snd3, r1, (p ^ 1, b))
    for i in range(LEAVES):
        st4[i] = stacked(skeleton_4(i))
    for i in range(LEAVES):
        field[i] = field[i] + apply_factor(st4[i], w3[i, pl.ds(0, LEAF)])
    third.wait_recv()
    tree = []
    for i in range(LEAVES):
        tree.append(field[i] + apply_factor(r1[places[4][i]], w3[i, pl.ds(LEAF, LEAF)]))
    for l in range(LEAVES):
        out_ref[:, pl.ds(l * LEAF, LEAF)] = lane_gather(tree, inv_w[pl.ds(l, 1), :], inv_l[pl.ds(l, 1), :]).astype(BF)
    for c in sends:
        c.wait_send()
    for there, _, copy, _ in halo:
        @pl.when(there)
        def _():
            copy.wait_send()


def on_device(points, tree_order, near, neighbours, compress, expand, top, mixers, block_map):
    skeleton = pltpu.VMEM((SENT, 2 * NV, LEAF), BF)
    n_copies = 8
    return pl.pallas_call(
        kernel,
        out_shape=pltpu.VMEM(points.shape, points.dtype),
        in_specs=[pl.BlockSpec(memory_space=pltpu.HBM)] * 9,
        out_specs=pl.BlockSpec(memory_space=pltpu.VMEM),
        scratch_shapes=[
            pltpu.VMEM(points.shape, BF), pltpu.VMEM((LEAVES, LEAF), jnp.int32), pltpu.VMEM(near.shape, BF),
            pltpu.VMEM(compress.shape, BF), pltpu.VMEM(expand.shape, BF), pltpu.VMEM(top.shape, BF),
            pltpu.VMEM(mixers.shape, BF), pltpu.SMEM(neighbours.shape[::-1], jnp.int32), pltpu.SMEM(block_map.shape, jnp.int32),
            pltpu.SMEM(block_map.shape, jnp.int32),
            pltpu.VMEM((LEAVES + 4, NV, LEAF), BF), pltpu.VMEM((LEAVES, NV, LEAF), F32),
            pltpu.VMEM((LEAVES, LEAF), jnp.int32), pltpu.VMEM((LEAVES, LEAF), jnp.int32),
            pltpu.VMEM((LEAVES, NV, LEAF), F32), pltpu.VMEM(points.shape, BF),
            skeleton, skeleton, skeleton,
            pltpu.VMEM((SENT, LEAF, LEAF), BF), pltpu.VMEM((SENT, LEAF, LEAF), BF),
            pltpu.VMEM((SENT, 2, LEAF, LEAF), BF), pltpu.VMEM((SENT, 2, LEAF, LEAF), BF),
            skeleton, skeleton, skeleton, skeleton, skeleton, skeleton, skeleton,
            pltpu.VMEM((LEAVES, 2 * LEAF, 2 * LEAF), BF), pltpu.VMEM((LEAVES, 4 * LEAF, 2 * LEAF), BF),
            pltpu.VMEM((LEAVES, 2 * LEAF, 2 * LEAF), BF),
            pltpu.VMEM((LEAVES, 2 * NV, LEAF), BF), pltpu.VMEM((LEAVES, 2 * NV, LEAF), BF),
            pltpu.SemaphoreType.DMA((10,)), pltpu.SemaphoreType.DMA((n_copies,)), pltpu.SemaphoreType.DMA((n_copies,)),
            pltpu.SemaphoreType.DMA((2,)), pltpu.SemaphoreType.DMA((2,)),
        ],
        compiler_params=pltpu.CompilerParams(collective_id=0, has_side_effects=True, vmem_limit_bytes=58 * 2**20),
        cost_estimate=pl.CostEstimate(flops=200_000_000, bytes_accessed=4_000_000, transcendentals=0),
        name="butterfly",
    )(points, tree_order.reshape(LEAVES, LEAF), near, neighbours.T, compress, expand, top, mixers, block_map)


def solution(mesh):
    both = ("partner", "block")
    return jax.shard_map(
        on_device,
        mesh=mesh,
        in_specs=(
            P(None, both),
            P(both),
            P(both, None, None, None),
            P(both, None),
            P(both, None, None),
            P(both, None, None),
            P(both, None, None),
            P(None, both, None, None, None),
            P(),
        ),
        out_specs=P(None, both),
        check_vma=False,
    )
```

time: 29.1 us -> 20.4 us (0.70)
  Pallas kernels: 27.5 us -> 19.7 us
  local copies, waits for them, and re-layouts: 1.47 us -> 0.63 us
    pallas_call x1, Pallas kernels: 27.5 us -> 19.7 us  [on_device(): pl.pallas_call(kernel, out_shape=pltpu.VMEM(points.shape, points.dtype),...]
    unnamed x1, local copies, waits for them, and re-layouts: 1.47 us -> 0.63 us
where the time goes in v2:
time: 20.4 us; the launch traced here: 20.3 us
  Pallas kernels  19.7 us (97%)
  local copies, waits for them, and re-layouts  0.63 us (3%)
    pallas_call x1, Pallas kernels, on_device(): pl.pallas_call(kernel, out_shape=pltpu.VMEM(points.shape, points.dtype),...  19.7 us
    unnamed x1, local copies, waits for them, and re-layouts  0.63 us

profile of v2, /device:TPU:1, one launch (start us, length us, event | category | flops | bytes accessed | tf_op | source)
XLA Modules:
  0.0 20.3 jit_solution(6643015216563813558)
XLA Ops:
  0.0 19.7 %butterfly.1 = bf16[32,1024]{1,0:T(8,128)(2,1)S(1)} custom-call(bf16[32,1024]{1,0:T(8,128)(2,1)} %points.1, s32[8,128]{1,0:T(8,128)} %bitcast.2, bf16[8,3,128,128]{3,2,1,0:T(8,128)(2,1)} %near.1, s32[3,8]{1,0:T(4,128)} %bitcast.3, bf16[8,128,128]{2,1,0:T(8,128)(2,1)} %compress.1, bf16[8,128,128]{2,1,0:T(8,128)(2,1)} %expand.1, bf16[8,128,128]{2,1,0:T(8,128)(2,1)} %top.1, ...), custom_call_target="tpu_custom_call" | custom-call | flops 200000000 | bytes 4000000 | tf_op jit(solution)/shard_map/butterfly/pallas_call | solution.py:260
  19.7 0.6 %copy.11 = bf16[32,1024]{1,0:T(8,128)(2,1)} copy(bf16[32,1024]{1,0:T(8,128)(2,1)S(1)} %butterfly.1) | data formatting | bytes 131072

commit v3 on v2

--- a/solution.py
+++ b/solution.py
@@ -36,6 +36,11 @@
 def apply_factor(x, w):
     y = dot(x, w)
     return (y[:NV, :LEAF] + y[NV:, :LEAF]) + y[:NV, LEAF:]
+
+
+def apply_exact(x, w):
+    y = dot(x, w)
+    return y[:NV] + y[NV:]
 
 
 def lane_gather(chunks, where, lane):
@@ -66,15 +71,14 @@
     win, field, inv_w, inv_l, acc, out_v,
     snd1, r16, r24, top8_s, top8_r, mix2_s, mix2_r,
     snd2a, snd2b, r4, r6, r2, snd3, r1,
-    w1, w2, w3, st2, st4,
-    load_sem, ssem, rsem, halo_ssem, halo_rsem,
+    w1, w2, w3, st2, st4, own1, part,
+    load_sem, ssem, rsem, halo_ssem, halo_rsem, entered,
 ):
     p = lax.axis_index("partner")
     b = lax.axis_index("block")
     n_b = lax.axis_size("block")
     me = p * n_b + b
     has_left, has_right = b > 0, b < n_b - 1
-    sides = ((has_left, b - 1), (has_right, b + 1))
 
     barrier = pltpu.get_barrier_semaphore()
     loads = {}
@@ -83,20 +87,23 @@
         loads[name] = pltpu.make_async_copy(src, dst, load_sem.at[k])
         loads[name].start()
 
-    partners = (16, 24, 8, 4, 6, 2, 1)
     load(0, "map", block_map, map_s)
     load(1, "order", order, ord_v)
-    for m in partners[:3]:
+    for m in (16, 24, 8):
         pl.semaphore_signal(barrier, inc=1, device_id=(p ^ m, b), device_id_type=MESH)
     load(2, "points", points, pts_v)
     load(3, "compress", compress, com_v)
     load(4, "top", top, top_v)
-    for m in partners[3:]:
-        pl.semaphore_signal(barrier, inc=1, device_id=(p ^ m, b), device_id_type=MESH)
-    for there, z in sides:
-        @pl.when(there)
+    late = (4, 6, 2, 1)
+    waits = [((p >> bit) & 1 == 1) != (p < 8) for bit in (2, 2, 1, 0)]
+    for m, waiter in zip(late, waits):
+        @pl.when(jnp.logical_not(waiter))
         def _():
-            pl.semaphore_signal(barrier, inc=1, device_id=(p, z), device_id_type=MESH)
+            pl.semaphore_signal(barrier, inc=1, device_id=(p ^ m, b), device_id_type=MESH)
+
+    @pl.when(has_right)
+    def _():
+        pl.semaphore_signal(barrier, inc=1, device_id=(p, b + 1), device_id_type=MESH)
     load(5, "mixers", mixers, mix_v)
     load(6, "expand", expand, exp_v)
     load(7, "near", near, near_v)
@@ -139,37 +146,53 @@
     for s in range(SENT):
         top8_s[s] = top_v[chosen[1][s]]
 
-    pl.semaphore_wait(barrier, len(partners) + has_left.astype(jnp.int32) + has_right.astype(jnp.int32))
+    pl.semaphore_wait(barrier, 3 + sum(w.astype(jnp.int32) for w in (has_left, *waits)))
     first = [send(snd1, r16, (p ^ 16, b)), send(snd1, r24, (p ^ 24, b))]
     top_copy = send(top8_s, top8_r, (p ^ 8, b))
+    for k, (m, waiter) in enumerate(zip(late, waits)):
+        @pl.when(waiter)
+        def _():
+            pl.semaphore_signal(entered.at[k], inc=1, device_id=(p ^ m, b), device_id_type=MESH)
+
+    def meet(k):
+        @pl.when(jnp.logical_not(waits[k]))
+        def _():
+            pl.semaphore_wait(entered.at[k], 1)
+
     for j in range(2, 5):
         tables(j)
     for l in range(LEAVES):
         row = ord_v[pl.ds(l, 1), :]
         win[l + 2] = lane_gather(chunks, (row >> 7) & 7, row & 127).astype(BF)
-    halo = []
-    for k, (there, z, src, dst) in enumerate(((*sides[1], LEAVES, 0), (*sides[0], 2, LEAVES + 2))):
-        copy = pltpu.make_async_remote_copy(
-            src_ref=win.at[pl.ds(src, 2)], dst_ref=win.at[pl.ds(dst, 2)], send_sem=halo_ssem.at[k],
-            recv_sem=halo_rsem.at[k], device_id=(p, z), device_id_type=MESH,
-        )
-        halo.append((there, sides[k][0], copy, dst))
-
-        @pl.when(there)
-        def _():
-            copy.start()
-
-        @pl.when(jnp.logical_not(sides[k][0]))
-        def _():
-            win[dst] = jnp.zeros((NV, LEAF), BF)
-            win[dst + 1] = jnp.zeros((NV, LEAF), BF)
+    to_left = pltpu.make_async_remote_copy(
+        src_ref=win.at[pl.ds(2, 2)], dst_ref=win.at[pl.ds(LEAVES + 2, 2)], send_sem=halo_ssem.at[0],
+        recv_sem=halo_rsem.at[0], device_id=(p, b - 1), device_id_type=MESH,
+    )
+    to_right = pltpu.make_async_remote_copy(
+        src_ref=win.at[pl.ds(LEAVES, 2)], dst_ref=win.at[pl.ds(0, 2)], send_sem=halo_ssem.at[1],
+        recv_sem=halo_rsem.at[1], device_id=(p, b + 1), device_id_type=MESH,
+    )
+
+    @pl.when(has_left)
+    def _():
+        pl.semaphore_signal(entered.at[4], inc=1, device_id=(p, b - 1), device_id_type=MESH)
+        to_left.start()
+
+    @pl.when(jnp.logical_not(has_left))
+    def _():
+        win[0] = jnp.zeros((NV, LEAF), BF)
+        win[1] = jnp.zeros((NV, LEAF), BF)
+
+    @pl.when(jnp.logical_not(has_right))
+    def _():
+        win[LEAVES + 2] = jnp.zeros((NV, LEAF), BF)
+        win[LEAVES + 3] = jnp.zeros((NV, LEAF), BF)
     loads["mixers"].wait()
     for s in range(SENT):
-        mix2_s[s] = mix_v[1, chosen[3][s]]
-    mix_copy = send(mix2_s, mix2_r, (p ^ 2, b))
-
-    for i in range(LEAVES):
-        w1[i, pl.ds(0, LEAF)] = paired(dot(top_v[i], mix_v[0, i, 0]))
+        mix2_s[s] = mix_v[1, chosen[3][s], 1]
+
+    for i in range(LEAVES):
+        w1[i] = paired(dot(top_v[i], mix_v[0, i, 0]))
     for i in range(LEAVES):
         w2[i, pl.ds(0, 2 * LEAF)] = paired(dot(mix_v[1, i].reshape(2 * LEAF, LEAF), mix_v[2, i, 0]))
     loads["expand"].wait()
@@ -190,24 +213,33 @@
     inv_w[...] = table[:LEAVES].astype(jnp.int32)
     inv_l[...] = table[LEAVES:].astype(jnp.int32)
 
-    top_copy.wait_recv()
-    for i in range(LEAVES):
-        w1[i, pl.ds(LEAF, LEAF)] = paired(dot(top8_r[places[1][i]], mix_v[0, i, 1]))
-
+    meet(2)
+    mix_copy = send(mix2_s, mix2_r, (p ^ 2, b))
     for c in first:
         c.wait_recv()
+    for i in range(LEAVES):
+        own1[i] = apply_factor(r16[places[0][i]], w1[i])
+    top_copy.wait_recv()
+    for s in range(SENT):
+        part[s] = stacked(apply_exact(r24[tab_s[0, chosen[1][s]]], top8_r[s]))
 
     def skeleton_2(c):
-        own = r16[tab_s[0, c]]
-        other = r24[tab_s[0, map_s[1, c]]]
-        return apply_factor(jnp.concatenate([own, other], axis=1), w1[c])
+        return own1[c] + apply_exact(part[tab_s[1, c]], mix_v[0, c, 1])
 
     for s in range(SENT):
         snd2a[s] = stacked(skeleton_2(chosen[2][s]))
+    meet(0)
+    meet(1)
     second = [send(snd2a, r4, (p ^ 4, b)), send(snd2a, r6, (p ^ 6, b))]
     for s in range(SENT):
-        snd2b[s] = stacked(skeleton_2(chosen[3][s]))
+        c = chosen[3][s]
+        snd2b[s] = stacked(apply_exact(stacked(skeleton_2(c)), mix_v[1, c, 0]))
     second.append(send(snd2b, r2, (p ^ 2, b)))
+    @pl.when(has_right)
+    def _():
+        pl.semaphore_wait(entered.at[4], 1)
+        to_right.start()
+
     for i in range(LEAVES):
         st2[i] = stacked(skeleton_2(i))
 
@@ -215,14 +247,17 @@
         acc[i] = apply_factor(st2[i], w2[i, pl.ds(0, LEAF)])
     mix_copy.wait_recv()
     for i in range(LEAVES):
-        other = mix2_r[places[3][i]].reshape(2 * LEAF, LEAF)
-        w2[i, pl.ds(2 * LEAF, 2 * LEAF)] = paired(dot(other, mix_v[2, i, 1]))
+        w2[i, pl.ds(2 * LEAF, LEAF)] = paired(dot(mix2_r[places[3][i]], mix_v[2, i, 1]))
     loads["near"].wait()
     loads["neighbours"].wait()
-    for _, comes, copy, _ in halo:
-        @pl.when(comes)
-        def _():
-            copy.wait_recv()
+    @pl.when(has_left)
+    def _():
+        to_right.wait_recv()
+
+    @pl.when(has_right)
+    def _():
+        to_left.wait_recv()
+
     for i in range(LEAVES):
         rows = jnp.concatenate([win[jnp.clip(near_s[n, i] - me * LEAVES + 2, 0, LEAVES + 3)] for n in range(3)], axis=1)
         field[i] = dot(rows, near_v[i].reshape(3 * LEAF, LEAF))
@@ -230,11 +265,13 @@
         c.wait_recv()
 
     def skeleton_4(c):
-        x = jnp.concatenate([r4[tab_s[2, c]], r2[tab_s[3, c]], r6[tab_s[2, map_s[3, c]]]], axis=1)
-        return acc[c] + apply_factor(x, w2[c, pl.ds(LEAF, 3 * LEAF)])
+        x = jnp.concatenate([r4[tab_s[2, c]], r6[tab_s[2, map_s[3, c]]]], axis=1)
+        y = acc[c] + apply_exact(r2[tab_s[3, c]], mix_v[2, c, 1])
+        return y + apply_factor(x, w2[c, pl.ds(LEAF, 2 * LEAF)])
 
     for s in range(SENT):
         snd3[s] = stacked(skeleton_4(chosen[4][s]))
+    meet(3)
     third = send(snd3, r1, (p ^ 1, b))
     for i in range(LEAVES):
         st4[i] = stacked(skeleton_4(i))
@@ -248,10 +285,13 @@
         out_ref[:, pl.ds(l * LEAF, LEAF)] = lane_gather(tree, inv_w[pl.ds(l, 1), :], inv_l[pl.ds(l, 1), :]).astype(BF)
     for c in sends:
         c.wait_send()
-    for there, _, copy, _ in halo:
-        @pl.when(there)
-        def _():
-            copy.wait_send()
+    @pl.when(has_left)
+    def _():
+        to_left.wait_send()
+
+    @pl.when(has_right)
+    def _():
+        to_right.wait_send()
 
 
 def on_device(points, tree_order, near, neighbours, compress, expand, top, mixers, block_map):
@@ -272,13 +312,14 @@
             pltpu.VMEM((LEAVES, NV, LEAF), F32), pltpu.VMEM(points.shape, BF),
             skeleton, skeleton, skeleton,
             pltpu.VMEM((SENT, LEAF, LEAF), BF), pltpu.VMEM((SENT, LEAF, LEAF), BF),
-            pltpu.VMEM((SENT, 2, LEAF, LEAF), BF), pltpu.VMEM((SENT, 2, LEAF, LEAF), BF),
+            pltpu.VMEM((SENT, LEAF, LEAF), BF), pltpu.VMEM((SENT, LEAF, LEAF), BF),
             skeleton, skeleton, skeleton, skeleton, skeleton, skeleton, skeleton,
-            pltpu.VMEM((LEAVES, 2 * LEAF, 2 * LEAF), BF), pltpu.VMEM((LEAVES, 4 * LEAF, 2 * LEAF), BF),
+            pltpu.VMEM((LEAVES, LEAF, 2 * LEAF), BF), pltpu.VMEM((LEAVES, 3 * LEAF, 2 * LEAF), BF),
             pltpu.VMEM((LEAVES, 2 * LEAF, 2 * LEAF), BF),
             pltpu.VMEM((LEAVES, 2 * NV, LEAF), BF), pltpu.VMEM((LEAVES, 2 * NV, LEAF), BF),
-            pltpu.SemaphoreType.DMA((10,)), pltpu.SemaphoreType.DMA((n_copies,)), pltpu.SemaphoreType.DMA((n_copies,)),
-            pltpu.SemaphoreType.DMA((2,)), pltpu.SemaphoreType.DMA((2,)),
+            pltpu.VMEM((LEAVES, NV, LEAF), F32), skeleton,
+            pltpu.SemaphoreType.DMA((9,)), pltpu.SemaphoreType.DMA((n_copies,)), pltpu.SemaphoreType.DMA((n_copies,)),
+            pltpu.SemaphoreType.DMA((2,)), pltpu.SemaphoreType.DMA((2,)), pltpu.SemaphoreType.REGULAR((5,)),
         ],
         compiler_params=pltpu.CompilerParams(collective_id=0, has_side_effects=True, vmem_limit_bytes=58 * 2**20),
         cost_estimate=pl.CostEstimate(flops=200_000_000, bytes_accessed=4_000_000, transcendentals=0),

time: 20.4 us -> 19.6 us (0.961)
  Pallas kernels: 19.7 us -> 18.8 us
    pallas_call x1, Pallas kernels: 19.7 us -> 18.8 us  [on_device(): pl.pallas_call(kernel, out_shape=pltpu.VMEM(points.shape, points.dtype),...]
where the time goes in v3:
time: 19.6 us; the launch traced here: 19.4 us
  Pallas kernels  18.8 us (96%)
  local copies, waits for them, and re-layouts  0.63 us (3%)
    pallas_call x1, Pallas kernels, on_device(): pl.pallas_call(kernel, out_shape=pltpu.VMEM(points.shape, points.dtype),...  18.8 us
    unnamed x1, local copies, waits for them, and re-layouts  0.63 us

profile of v3, /device:TPU:1, one launch (start us, length us, event | category | flops | bytes accessed | tf_op | source)
XLA Modules:
  0.0 19.4 jit_solution(12761435100660168301)
XLA Ops:
  0.0 18.8 %butterfly.1 = bf16[32,1024]{1,0:T(8,128)(2,1)S(1)} custom-call(bf16[32,1024]{1,0:T(8,128)(2,1)} %points.1, s32[8,128]{1,0:T(8,128)} %bitcast.2, bf16[8,3,128,128]{3,2,1,0:T(8,128)(2,1)} %near.1, s32[3,8]{1,0:T(4,128)} %bitcast.3, bf16[8,128,128]{2,1,0:T(8,128)(2,1)} %compress.1, bf16[8,128,128]{2,1,0:T(8,128)(2,1)} %expand.1, bf16[8,128,128]{2,1,0:T(8,128)(2,1)} %top.1, ...), custom_call_target="tpu_custom_call" | custom-call | flops 200000000 | bytes 4000000 | tf_op jit(solution)/shard_map/butterfly/pallas_call | solution.py:300
  18.8 0.6 %copy.11 = bf16[32,1024]{1,0:T(8,128)(2,1)} copy(bf16[32,1024]{1,0:T(8,128)(2,1)S(1)} %butterfly.1) | data formatting | bytes 131072

commit v4 on v3

--- a/solution.py
+++ b/solution.py
@@ -68,9 +68,9 @@
     points, order, near, neighbours, compress, expand, top, mixers, block_map,
     out_ref,
     pts_v, ord_v, near_v, com_v, exp_v, top_v, mix_v, near_s, map_s, tab_s,
-    win, field, inv_w, inv_l, acc, out_v,
-    snd1, r16, r24, top8_s, top8_r, mix2_s, mix2_r,
-    snd2a, snd2b, r4, r6, r2, snd3, r1,
+    win, field, inv_w, inv_l, acc,
+    snd1, rec1, top8_s, top8_r, mix2_s, mix2_r,
+    snd2a, snd2b, rec2, snd3, r1,
     w1, w2, w3, st2, st4, own1, part,
     load_sem, ssem, rsem, halo_ssem, halo_rsem, entered,
 ):
@@ -87,13 +87,16 @@
         loads[name] = pltpu.make_async_copy(src, dst, load_sem.at[k])
         loads[name].start()
 
+    def arrived(part, sem):
+        pltpu.make_async_copy(part, part, sem).wait()
+
     load(0, "map", block_map, map_s)
     load(1, "order", order, ord_v)
     for m in (16, 24, 8):
         pl.semaphore_signal(barrier, inc=1, device_id=(p ^ m, b), device_id_type=MESH)
     load(2, "points", points, pts_v)
-    load(3, "compress", compress, com_v)
-    load(4, "top", top, top_v)
+    load(2, "compress", compress, com_v)
+    load(2, "top", top, top_v)
     late = (4, 6, 2, 1)
     waits = [((p >> bit) & 1 == 1) != (p < 8) for bit in (2, 2, 1, 0)]
     for m, waiter in zip(late, waits):
@@ -104,22 +107,17 @@
     @pl.when(has_right)
     def _():
         pl.semaphore_signal(barrier, inc=1, device_id=(p, b + 1), device_id_type=MESH)
-    load(5, "mixers", mixers, mix_v)
-    load(6, "expand", expand, exp_v)
-    load(7, "near", near, near_v)
-    load(8, "neighbours", neighbours, near_s)
-
-    used = [0]
-    sends = []
-
-    def send(src, dst, to):
-        k = used[0]
-        used[0] += 1
+    load(3, "mixers", mixers, mix_v)
+    load(4, "expand", expand, exp_v)
+    load(4, "near", near, near_v)
+    load(5, "neighbours", neighbours, near_s)
+
+
+    def send(k, src, dst, to):
         c = pltpu.make_async_remote_copy(
-            src_ref=src, dst_ref=dst, send_sem=ssem.at[k], recv_sem=rsem.at[k], device_id=to, device_id_type=MESH
+            src_ref=src, dst_ref=dst, send_sem=ssem.at[0], recv_sem=rsem.at[k], device_id=to, device_id_type=MESH
         )
         c.start()
-        sends.append(c)
         return c
 
     loads["map"].wait()
@@ -131,24 +129,22 @@
             tab_s[j, i] = places[j][i]
 
     tables(0)
-    tables(1)
 
     loads["order"].wait()
-    loads["points"].wait()
+    arrived(mix_v.at[pl.ds(0, 3), pl.ds(0, 3)], load_sem.at[2])
     chunks = [pts_v[:, pl.ds(k * LEAF, LEAF)].astype(F32) for k in range(LEAVES)]
-    loads["compress"].wait()
     for s in range(SENT):
         c = chosen[0][s]
         row = ord_v[pl.ds(c, 1), :]
         rows = lane_gather(chunks, (row >> 7) & 7, row & 127).astype(BF)
         snd1[s] = stacked(dot(rows, com_v[c]))
-    loads["top"].wait()
+    pl.semaphore_wait(barrier, 3 + sum(w.astype(jnp.int32) for w in (has_left, *waits)))
+    send(0, snd1, rec1.at[1], (p ^ 24, b))
+    send(0, snd1, rec1.at[0], (p ^ 16, b))
+    tables(1)
     for s in range(SENT):
         top8_s[s] = top_v[chosen[1][s]]
-
-    pl.semaphore_wait(barrier, 3 + sum(w.astype(jnp.int32) for w in (has_left, *waits)))
-    first = [send(snd1, r16, (p ^ 16, b)), send(snd1, r24, (p ^ 24, b))]
-    top_copy = send(top8_s, top8_r, (p ^ 8, b))
+    top_copy = send(1, top8_s, top8_r, (p ^ 8, b))
     for k, (m, waiter) in enumerate(zip(late, waits)):
         @pl.when(waiter)
         def _():
@@ -195,7 +191,7 @@
         w1[i] = paired(dot(top_v[i], mix_v[0, i, 0]))
     for i in range(LEAVES):
         w2[i, pl.ds(0, 2 * LEAF)] = paired(dot(mix_v[1, i].reshape(2 * LEAF, LEAF), mix_v[2, i, 0]))
-    loads["expand"].wait()
+    arrived(mix_v.at[pl.ds(0, 2)], load_sem.at[4])
     for i in range(LEAVES):
         w3[i] = paired(dot(mix_v[3, i].reshape(2 * LEAF, LEAF), exp_v[i]))
     sub = lax.broadcasted_iota(jnp.int32, (LEAVES, LEAF), 0)
@@ -214,14 +210,13 @@
     inv_l[...] = table[LEAVES:].astype(jnp.int32)
 
     meet(2)
-    mix_copy = send(mix2_s, mix2_r, (p ^ 2, b))
-    for c in first:
-        c.wait_recv()
-    for i in range(LEAVES):
-        own1[i] = apply_factor(r16[places[0][i]], w1[i])
+    mix_copy = send(2, mix2_s, mix2_r, (p ^ 2, b))
+    arrived(rec1, rsem.at[0])
+    for i in range(LEAVES):
+        own1[i] = apply_factor(rec1[0, places[0][i]], w1[i])
     top_copy.wait_recv()
     for s in range(SENT):
-        part[s] = stacked(apply_exact(r24[tab_s[0, chosen[1][s]]], top8_r[s]))
+        part[s] = stacked(apply_exact(rec1[1, tab_s[0, chosen[1][s]]], top8_r[s]))
 
     def skeleton_2(c):
         return own1[c] + apply_exact(part[tab_s[1, c]], mix_v[0, c, 1])
@@ -230,11 +225,12 @@
         snd2a[s] = stacked(skeleton_2(chosen[2][s]))
     meet(0)
     meet(1)
-    second = [send(snd2a, r4, (p ^ 4, b)), send(snd2a, r6, (p ^ 6, b))]
+    send(3, snd2a, rec2.at[1], (p ^ 6, b))
+    send(3, snd2a, rec2.at[0], (p ^ 4, b))
     for s in range(SENT):
         c = chosen[3][s]
         snd2b[s] = stacked(apply_exact(stacked(skeleton_2(c)), mix_v[1, c, 0]))
-    second.append(send(snd2b, r2, (p ^ 2, b)))
+    send(3, snd2b, rec2.at[2], (p ^ 2, b))
     @pl.when(has_right)
     def _():
         pl.semaphore_wait(entered.at[4], 1)
@@ -248,7 +244,6 @@
     mix_copy.wait_recv()
     for i in range(LEAVES):
         w2[i, pl.ds(2 * LEAF, LEAF)] = paired(dot(mix2_r[places[3][i]], mix_v[2, i, 1]))
-    loads["near"].wait()
     loads["neighbours"].wait()
     @pl.when(has_left)
     def _():
@@ -261,18 +256,17 @@
     for i in range(LEAVES):
         rows = jnp.concatenate([win[jnp.clip(near_s[n, i] - me * LEAVES + 2, 0, LEAVES + 3)] for n in range(3)], axis=1)
         field[i] = dot(rows, near_v[i].reshape(3 * LEAF, LEAF))
-    for c in second:
-        c.wait_recv()
+    arrived(rec2, rsem.at[3])
 
     def skeleton_4(c):
-        x = jnp.concatenate([r4[tab_s[2, c]], r6[tab_s[2, map_s[3, c]]]], axis=1)
-        y = acc[c] + apply_exact(r2[tab_s[3, c]], mix_v[2, c, 1])
+        x = jnp.concatenate([rec2[0, tab_s[2, c]], rec2[1, tab_s[2, map_s[3, c]]]], axis=1)
+        y = acc[c] + apply_exact(rec2[2, tab_s[3, c]], mix_v[2, c, 1])
         return y + apply_factor(x, w2[c, pl.ds(LEAF, 2 * LEAF)])
 
     for s in range(SENT):
         snd3[s] = stacked(skeleton_4(chosen[4][s]))
     meet(3)
-    third = send(snd3, r1, (p ^ 1, b))
+    third = send(4, snd3, r1, (p ^ 1, b))
     for i in range(LEAVES):
         st4[i] = stacked(skeleton_4(i))
     for i in range(LEAVES):
@@ -283,8 +277,7 @@
         tree.append(field[i] + apply_factor(r1[places[4][i]], w3[i, pl.ds(LEAF, LEAF)]))
     for l in range(LEAVES):
         out_ref[:, pl.ds(l * LEAF, LEAF)] = lane_gather(tree, inv_w[pl.ds(l, 1), :], inv_l[pl.ds(l, 1), :]).astype(BF)
-    for c in sends:
-        c.wait_send()
+    arrived(mix_v.at[pl.ds(0, 2), pl.ds(0, 5)], ssem.at[0])
     @pl.when(has_left)
     def _():
         to_left.wait_send()
@@ -296,7 +289,10 @@
 
 def on_device(points, tree_order, near, neighbours, compress, expand, top, mixers, block_map):
     skeleton = pltpu.VMEM((SENT, 2 * NV, LEAF), BF)
-    n_copies = 8
+
+    def received(count):
+        return pltpu.VMEM((count, SENT, 2 * NV, LEAF), BF)
+
     return pl.pallas_call(
         kernel,
         out_shape=pltpu.VMEM(points.shape, points.dtype),
@@ -309,16 +305,16 @@
             pltpu.SMEM(block_map.shape, jnp.int32),
             pltpu.VMEM((LEAVES + 4, NV, LEAF), BF), pltpu.VMEM((LEAVES, NV, LEAF), F32),
             pltpu.VMEM((LEAVES, LEAF), jnp.int32), pltpu.VMEM((LEAVES, LEAF), jnp.int32),
-            pltpu.VMEM((LEAVES, NV, LEAF), F32), pltpu.VMEM(points.shape, BF),
-            skeleton, skeleton, skeleton,
+            pltpu.VMEM((LEAVES, NV, LEAF), F32),
+            skeleton, received(2),
             pltpu.VMEM((SENT, LEAF, LEAF), BF), pltpu.VMEM((SENT, LEAF, LEAF), BF),
             pltpu.VMEM((SENT, LEAF, LEAF), BF), pltpu.VMEM((SENT, LEAF, LEAF), BF),
-            skeleton, skeleton, skeleton, skeleton, skeleton, skeleton, skeleton,
+            skeleton, skeleton, received(3), skeleton, skeleton,
             pltpu.VMEM((LEAVES, LEAF, 2 * LEAF), BF), pltpu.VMEM((LEAVES, 3 * LEAF, 2 * LEAF), BF),
             pltpu.VMEM((LEAVES, 2 * LEAF, 2 * LEAF), BF),
             pltpu.VMEM((LEAVES, 2 * NV, LEAF), BF), pltpu.VMEM((LEAVES, 2 * NV, LEAF), BF),
             pltpu.VMEM((LEAVES, NV, LEAF), F32), skeleton,
-            pltpu.SemaphoreType.DMA((9,)), pltpu.SemaphoreType.DMA((n_copies,)), pltpu.SemaphoreType.DMA((n_copies,)),
+            pltpu.SemaphoreType.DMA((6,)), pltpu.SemaphoreType.DMA((1,)), pltpu.SemaphoreType.DMA((5,)),
             pltpu.SemaphoreType.DMA((2,)), pltpu.SemaphoreType.DMA((2,)), pltpu.SemaphoreType.REGULAR((5,)),
         ],
         compiler_params=pltpu.CompilerParams(collective_id=0, has_side_effects=True, vmem_limit_bytes=58 * 2**20),

time: 19.6 us -> 19.5 us (level)
  no operation moved by 1% of the time
where the time goes in v4:
time: 19.5 us; the launch traced here: 19.3 us
  Pallas kernels  18.7 us (96%)
  local copies, waits for them, and re-layouts  0.63 us (3%)
    pallas_call x1, Pallas kernels, on_device(): pl.pallas_call(kernel, out_shape=pltpu.VMEM(points.shape, points.dtype),...  18.7 us
    unnamed x1, local copies, waits for them, and re-layouts  0.63 us

profile of v4, /device:TPU:1, one launch (start us, length us, event | category | flops | bytes accessed | tf_op | source)
XLA Modules:
  0.0 19.3 jit_solution(9892367947707348810)
XLA Ops:
  0.0 18.7 %butterfly.1 = bf16[32,1024]{1,0:T(8,128)(2,1)S(1)} custom-call(bf16[32,1024]{1,0:T(8,128)(2,1)} %points.1, s32[8,128]{1,0:T(8,128)} %bitcast.2, bf16[8,3,128,128]{3,2,1,0:T(8,128)(2,1)} %near.1, s32[3,8]{1,0:T(4,128)} %bitcast.3, bf16[8,128,128]{2,1,0:T(8,128)(2,1)} %compress.1, bf16[8,128,128]{2,1,0:T(8,128)(2,1)} %expand.1, bf16[8,128,128]{2,1,0:T(8,128)(2,1)} %top.1, ...), custom_call_target="tpu_custom_call" | custom-call | flops 200000000 | bytes 4000000 | tf_op jit(solution)/shard_map/butterfly/pallas_call | solution.py:296
  18.7 0.6 %copy.11 = bf16[32,1024]{1,0:T(8,128)(2,1)} copy(bf16[32,1024]{1,0:T(8,128)(2,1)S(1)} %butterfly.1) | data formatting | bytes 131072

commit v5 on v4

--- a/solution.py
+++ b/solution.py
@@ -107,10 +107,6 @@
     @pl.when(has_right)
     def _():
         pl.semaphore_signal(barrier, inc=1, device_id=(p, b + 1), device_id_type=MESH)
-    load(3, "mixers", mixers, mix_v)
-    load(4, "expand", expand, exp_v)
-    load(4, "near", near, near_v)
-    load(5, "neighbours", neighbours, near_s)
 
 
     def send(k, src, dst, to):
@@ -132,6 +128,10 @@
 
     loads["order"].wait()
     arrived(mix_v.at[pl.ds(0, 3), pl.ds(0, 3)], load_sem.at[2])
+    load(3, "mixers", mixers, mix_v)
+    load(4, "expand", expand, exp_v)
+    load(4, "near", near, near_v)
+    load(5, "neighbours", neighbours, near_s)
     chunks = [pts_v[:, pl.ds(k * LEAF, LEAF)].astype(F32) for k in range(LEAVES)]
     for s in range(SENT):
         c = chosen[0][s]

time: 19.5 us -> 19.5 us (level)
  no operation moved by 1% of the time
where the time goes in v5:
time: 19.5 us; the launch traced here: 19.3 us
  Pallas kernels  18.7 us (96%)
  local copies, waits for them, and re-layouts  0.63 us (3%)
    pallas_call x1, Pallas kernels, on_device(): pl.pallas_call(kernel, out_shape=pltpu.VMEM(points.shape, points.dtype),...  18.7 us
    unnamed x1, local copies, waits for them, and re-layouts  0.63 us

profile of v5, /device:TPU:1, one launch (start us, length us, event | category | flops | bytes accessed | tf_op | source)
XLA Modules:
  0.0 19.3 jit_solution(1623316106109957909)
XLA Ops:
  0.0 18.7 %butterfly.1 = bf16[32,1024]{1,0:T(8,128)(2,1)S(1)} custom-call(bf16[32,1024]{1,0:T(8,128)(2,1)} %points.1, s32[8,128]{1,0:T(8,128)} %bitcast.2, bf16[8,3,128,128]{3,2,1,0:T(8,128)(2,1)} %near.1, s32[3,8]{1,0:T(4,128)} %bitcast.3, bf16[8,128,128]{2,1,0:T(8,128)(2,1)} %compress.1, bf16[8,128,128]{2,1,0:T(8,128)(2,1)} %expand.1, bf16[8,128,128]{2,1,0:T(8,128)(2,1)} %top.1, ...), custom_call_target="tpu_custom_call" | custom-call | flops 200000000 | bytes 4000000 | tf_op jit(solution)/shard_map/butterfly/pallas_call | solution.py:296
  18.7 0.6 %copy.11 = bf16[32,1024]{1,0:T(8,128)(2,1)} copy(bf16[32,1024]{1,0:T(8,128)(2,1)S(1)} %butterfly.1) | data formatting | bytes 131072
